TPU v7x, 32 devices: a whole 2x2x4 slice. The times are simulated.
32 devices in a mesh: tm: 4 (over z), height: 8 (over y, x, core).
Axes of the slice: x: 2, y: 2, z: 4, core: 2. Of those that a mesh axis runs over, the one named last changes fastest.
Arguments:
- latents: bfloat16 [9, 16, 128, 384], P(None, 'height', 'tm'), may hold values from -6 to 6
- gain_in: float32 [384], replicated, may hold values from 0.1 to 1.9
- weight_in: bfloat16 [3, 3, 3, 384, 384], replicated, may hold values from -0.0625 to 0.0625
- bias_in: float32 [384], replicated, may hold values from -3 to 3
- gain_mid: float32 [384], replicated, may hold values from 0.1 to 1.9
- weight_mid: bfloat16 [3, 3, 3, 384, 384], replicated, may hold values from -0.0625 to 0.0625
- bias_mid: float32 [384], replicated, may hold values from -2 to 2
- up_weight: bfloat16 [3, 3, 384, 192], replicated, may hold values from -0.109375 to 0.109375
- up_bias: float32 [192], replicated, may hold values from -2 to 2
Outputs:
- first_image: bfloat16 [32, 256, 192], P('height', 'tm')
- later_images: bfloat16 [8, 32, 256, 192], P('tm', 'height')
All inputs are finite; a program needn't handle non-finite values.
Results may differ from a plain program's by a relative error of at most 0.0053.
Values may be sent and summed in bfloat16 or wider, within the bound.
A program may use at most 128 MiB of HBM per device.

v0:
```python
import jax
import jax.numpy as jnp
from jax import lax
from jax.sharding import PartitionSpec as P

epsilon = 1e-06


def with_halo(array, sides, width):
    for axis, dim in sides:
        peers, length = (lax.axis_size(axis), array.shape[dim])
        up = [(i, (i + 1) % peers) for i in range(peers - 1)]
        down = [(j, i) for i, j in up]
        last = lax.slice_in_dim(array, length - width, length, axis=dim)
        leading = lax.slice_in_dim(array, 0, width, axis=dim)
        before = lax.ppermute(last, axis, up)
        after = lax.ppermute(leading, axis, down)
        array = jnp.concatenate([before, array, after], axis=dim)
    return array


def normed_silu(values, norm_gain):
    factor = lax.rsqrt(jnp.mean(values * values, axis=-1, keepdims=True) + epsilon)
    return jax.nn.silu(values * factor * norm_gain)


def column_pad(values):
    pad_spec = [(0, 0)] * (values.ndim - 2) + [(1, 1), (0, 0)]
    return jnp.pad(values, pad_spec)


def row_taps(slab_rows, tap_weights):
    col_count = slab_rows.shape[-2] - 2
    widened = jnp.concatenate(
        [slab_rows[..., offset : offset + col_count, :] for offset in range(3)], axis=-1
    )
    merged = tap_weights.reshape(3 * tap_weights.shape[1], tap_weights.shape[2])
    return jnp.einsum("...c,cd->...d", widened, merged, preferred_element_type=jnp.float32)


def plane_conv(padded, tap_weights):
    row_count = padded.shape[-3] - 2
    summed = row_taps(padded[..., 0:row_count, :, :], tap_weights[0])
    for offset in range(1, 3):
        summed = summed + row_taps(
            padded[..., offset : offset + row_count, :, :], tap_weights[offset]
        )
    return summed


def causal_conv(padded, weight):
    frame_count = padded.shape[0] - 2
    summed = plane_conv(padded[0:frame_count], weight[0])
    for offset in range(1, 3):
        summed = summed + plane_conv(padded[offset : offset + frame_count], weight[offset])
    return summed


def enlarge_conv(framed, tap_weights, col_start, col_count):
    doubled = jnp.repeat(jnp.repeat(framed, 2, axis=-3), 2, axis=-2)
    doubled = doubled[..., 1:-1, :, :]
    window = lax.dynamic_slice_in_dim(doubled, col_start + 1, col_count + 2, axis=doubled.ndim - 2)
    return plane_conv(window, tap_weights)


def brick_pad(values):
    rimmed = with_halo(values, (("tm", 2), ("height", 1)), 1)
    return jnp.pad(rimmed, ((2, 0), (0, 0), (0, 0), (0, 0)))


def body(latents, gain_in, weight_in, bias_in, gain_mid, weight_mid, bias_mid, up_weight, up_bias):
    groups = lax.axis_size("tm")
    frames_all, row_count, quarter, channels = latents.shape
    width_all = quarter * groups
    widened = latents.astype(jnp.float32)
    inner = normed_silu(widened, gain_in).astype(jnp.bfloat16)
    mixed = causal_conv(brick_pad(inner), weight_in) + bias_in
    middle = normed_silu(mixed, gain_mid).astype(jnp.bfloat16)
    result = causal_conv(brick_pad(middle), weight_mid) + bias_mid
    summed = (widened + result).astype(jnp.bfloat16)
    first_rimmed = with_halo(summed[0], (("tm", 1), ("height", 0)), 1)
    first_image = (enlarge_conv(first_rimmed, up_weight, 0, 2 * quarter) + up_bias).astype(
        jnp.bfloat16
    )
    later_block = lax.all_to_all(summed[1:], "tm", split_axis=0, concat_axis=2, tiled=True)
    later_in = column_pad(with_halo(later_block, (("height", 1),), 1))
    later_images = (enlarge_conv(later_in, up_weight, 0, 2 * width_all) + up_bias).astype(
        jnp.bfloat16
    )
    return (first_image, later_images)


def solution(mesh):
    return jax.shard_map(
        body,
        mesh=mesh,
        in_specs=(P(None, "height", "tm", None), P(), P(), P(), P(), P(), P(), P(), P()),
        out_specs=(P("height", "tm", None), P("tm", "height", None, None)),
        check_vma=False,
    )
```

profile of v0, /device:TPU:1, one launch (start us, length us, event | category | flops | bytes accessed | tf_op | source)
XLA Modules:
  0.0 134.4 jit_solution(5476568254930311724)
XLA Ops:
  0.6 1.2 fusion.211
  1.8 1.4 %fusion.218 = bf16[9,2,32,384]{3,2,1,0:T(8,128)(2,1)S(1)} fusion(bf16[9,2,32,384]{3,2,1,0:T(8,128)(2,1)} %param.9, f32[384]{0:T(512)} %param.10, f32[9,2,32]{2,1,0:T(2,128)S(1)} %add_rsqrt_fusion.1), kind=kLoop, calls=%fused_computation.183 | loop fusion | flops 1769472 | bytes 888576 | tf_op jit(solution)/shard_map/convert_element_type | solution.py:76
  3.2 4.0 %collective-permute-start = (bf16[9,2,1,384]{3,2,1,0:T(2,128)(2,1)S(1)}, bf16[9,2,1,384]{3,2,1,0:T(2,128)(2,1)S(1)}, u32[]{:S(2)}, u32[]{:S(2)}) collective-permute-start(bf16[9,2,1,384]{3,2,1,0:T(2,128)(2,1)S(1)} %get-tuple-element.90), channel_id=1, source_target_pairs={{0,8},{8,16},{16,24},{1,9},{9,17},{17,25},{2,10},{10,18},{18,26},{... | collective-permute-start | bytes 41480 | tf_op jit(solution)/shard_map/ppermute | solution.py:16
  7.3 1.3 collective-permute-start.1
  8.6 3.8 %fusion.263 = (bf16[1,1,3,384,384]{4,3,2,1,0:T(8,128)(2,1)S(1)}, bf16[1,1,3,384,384]{4,3,2,1,0:T(8,128)(2,1)S(1)}, bf16[1,1,3,384,384]{4,3,2,1,0:T(8,128)(2,1)S(...) fusion(bf16[3,3,3,384,384]{4,3,2,1,0:T(8,128)(2,1)} %param.11), kind=kLoop, calls=%fused_computation.242 | loop fusion | bytes 15925248 | tf_op jit(solution)/shard_map/slice | solution.py:43
  12.8 4.6 %collective-permute-start.2 = (bf16[9,1,34,384]{3,2,1,0:T(8,128)(2,1)S(1)}, bf16[9,1,34,384]{3,2,1,0:T(8,128)(2,1)S(1)}, u32[]{:S(2)}, u32[]{:S(2)}) collective-permute-start(bf16[9,1,34,384]{3,2,1,0:T(8,128)(2,1)S(1)} %get-tuple-element.82), channel_id=1, source_target_pairs={{0,1},{1,2},{2,3},{3,4},{4,5},{5,6},{6,7},{8,9},{9,10},{10,11},{11... | collective-permute-start | bytes 705032 | tf_op jit(solution)/shard_map/ppermute | solution.py:16
  17.3 1.9 %collective-permute-start.3 = (bf16[9,1,34,384]{3,2,1,0:T(8,128)(2,1)S(1)}, bf16[9,1,34,384]{3,2,1,0:T(8,128)(2,1)S(1)}, u32[]{:S(2)}, u32[]{:S(2)}) collective-permute-start(bf16[9,1,34,384]{3,2,1,0:T(8,128)(2,1)S(1)} %get-tuple-element.83), channel_id=1, source_target_pairs={{1,0},{2,1},{3,2},{4,3},{5,4},{6,5},{7,6},{9,8},{10,9},{11,10},{12... | collective-permute-start | bytes 705032 | tf_op jit(solution)/shard_map/ppermute | solution.py:17
  20.8 4.6 %collective-permute-done.3 = bf16[9,1,34,384]{3,2,1,0:T(8,128)(2,1)S(1)} collective-permute-done((bf16[9,1,34,384]{3,2,1,0:T(8,128)(2,1)S(1)}, bf16[9,1,34,384]{3,2,1,0:T(8,128)(2,1)S(1)}, u32[]{:S(2)}, u32[]{:S(2)}) %collective-permute-start.3) | collective-permute-done | bytes 235040 | tf_op jit(solution)/shard_map/ppermute | solution.py:17
  25.7 1.8 %fusion.266 = (bf16[9,2,32,384]{3,2,1,0:T(8,128)(2,1)S(1)}, bf16[9,2,32,384]{3,2,1,0:T(8,128)(2,1)S(1)}, bf16[9,2,32,384]{3,2,1,0:T(8,128)(2,1)S(1)}, bf16[9,2,3...) fusion(bf16[11,4,34,384]{3,2,1,0:T(8,128)(2,1)S(1)} %fusion.33), kind=kLoop, calls=%fused_computation.245 | loop fusion | bytes 15925248 | tf_op jit(solution)/shard_map/slice | solution.py:35
  36.5 3.7 %collective-permute-start.4 = (bf16[9,2,1,384]{3,2,1,0:T(2,128)(2,1)S(1)}, bf16[9,2,1,384]{3,2,1,0:T(2,128)(2,1)S(1)}, u32[]{:S(2)}, u32[]{:S(2)}) collective-permute-start(bf16[9,2,1,384]{3,2,1,0:T(2,128)(2,1)S(1)} %get-tuple-element.88), channel_id=1, source_target_pairs={{0,8},{8,16},{16,24},{1,9},{9,17},{17,25},{2,10},{10,18},{18,26},{... | collective-permute-start | bytes 41480 | tf_op jit(solution)/shard_map/ppermute | solution.py:16
  40.2 1.3 collective-permute-start.5
  42.6 2.1 %collective-permute-done.5 = bf16[9,2,1,384]{3,2,1,0:T(2,128)(2,1)S(1)} collective-permute-done((bf16[9,2,1,384]{3,2,1,0:T(2,128)(2,1)S(1)}, bf16[9,2,1,384]{3,2,1,0:T(2,128)(2,1)S(1)}, u32[]{:S(2)}, u32[]{:S(2)}) %collective-permute-start.5) | collective-permute-done | bytes 13856 | tf_op jit(solution)/shard_map/ppermute | solution.py:17
  45.1 3.2 %collective-permute-start.6 = (bf16[9,1,34,384]{3,2,1,0:T(8,128)(2,1)S(1)}, bf16[9,1,34,384]{3,2,1,0:T(8,128)(2,1)S(1)}, u32[]{:S(2)}, u32[]{:S(2)}) collective-permute-start(bf16[9,1,34,384]{3,2,1,0:T(8,128)(2,1)S(1)} %get-tuple-element.80), channel_id=1, source_target_pairs={{0,1},{1,2},{2,3},{3,4},{4,5},{5,6},{6,7},{8,9},{9,10},{10,11},{11... | collective-permute-start | bytes 705032 | tf_op jit(solution)/shard_map/ppermute | solution.py:16
  48.3 2.1 %collective-permute-start.7 = (bf16[9,1,34,384]{3,2,1,0:T(8,128)(2,1)S(1)}, bf16[9,1,34,384]{3,2,1,0:T(8,128)(2,1)S(1)}, u32[]{:S(2)}, u32[]{:S(2)}) collective-permute-start(bf16[9,1,34,384]{3,2,1,0:T(8,128)(2,1)S(1)} %get-tuple-element.81), channel_id=1, source_target_pairs={{1,0},{2,1},{3,2},{4,3},{5,4},{6,5},{7,6},{9,8},{10,9},{11,10},{12... | collective-permute-start | bytes 705032 | tf_op jit(solution)/shard_map/ppermute | solution.py:17
  51.7 5.3 %collective-permute-done.7 = bf16[9,1,34,384]{3,2,1,0:T(8,128)(2,1)S(1)} collective-permute-done((bf16[9,1,34,384]{3,2,1,0:T(8,128)(2,1)S(1)}, bf16[9,1,34,384]{3,2,1,0:T(8,128)(2,1)S(1)}, u32[]{:S(2)}, u32[]{:S(2)}) %collective-permute-start.7) | collective-permute-done | bytes 235040 | tf_op jit(solution)/shard_map/ppermute | solution.py:17
  57.4 1.7 %fusion.265 = (bf16[9,2,32,384]{3,2,1,0:T(8,128)(2,1)S(1)}, bf16[9,2,32,384]{3,2,1,0:T(8,128)(2,1)S(1)}, bf16[9,2,32,384]{3,2,1,0:T(8,128)(2,1)S(1)}, bf16[9,2,3...) fusion(bf16[11,4,34,384]{3,2,1,0:T(8,128)(2,1)S(1)} %fusion.31), kind=kLoop, calls=%fused_computation.244 | loop fusion | bytes 15925248 | tf_op jit(solution)/shard_map/slice | solution.py:35
  67.4 3.2 %collective-permute-start.8 = (bf16[2,1,384]{2,1,0:T(2,128)(2,1)S(1)}, bf16[2,1,384]{2,1,0:T(2,128)(2,1)S(1)}, u32[]{:S(2)}, u32[]{:S(2)}) collective-permute-start(bf16[2,1,384]{2,1,0:T(2,128)(2,1)S(1)} %get-tuple-element.105), channel_id=1, source_target_pairs={{0,8},{8,16},{16,24},{1,9},{9,17},{17,25},{2,10},{10,18},{18,26},{... | collective-permute-start | bytes 4616 | tf_op jit(solution)/shard_map/ppermute | solution.py:16
  70.6 1.3 collective-permute-start.9
  71.9 3.0 %collective-permute-done.9 = bf16[2,1,384]{2,1,0:T(2,128)(2,1)S(1)} collective-permute-done((bf16[2,1,384]{2,1,0:T(2,128)(2,1)S(1)}, bf16[2,1,384]{2,1,0:T(2,128)(2,1)S(1)}, u32[]{:S(2)}, u32[]{:S(2)}) %collective-permute-start.9) | collective-permute-done | bytes 1568 | tf_op jit(solution)/shard_map/ppermute | solution.py:17
  75.0 3.2 %collective-permute-start.10 = (bf16[1,34,384]{2,1,0:T(8,128)(2,1)S(1)}, bf16[1,34,384]{2,1,0:T(8,128)(2,1)S(1)}, u32[]{:S(2)}, u32[]{:S(2)}) collective-permute-start(bf16[1,34,384]{2,1,0:T(8,128)(2,1)S(1)} %get-tuple-element.103), channel_id=1, source_target_pairs={{0,1},{1,2},{2,3},{3,4},{4,5},{5,6},{6,7},{8,9},{9,10},{10,11},{11... | collective-permute-start | bytes 78344 | tf_op jit(solution)/shard_map/ppermute | solution.py:16
  78.2 1.9 %collective-permute-start.11 = (bf16[1,34,384]{2,1,0:T(8,128)(2,1)S(1)}, bf16[1,34,384]{2,1,0:T(8,128)(2,1)S(1)}, u32[]{:S(2)}, u32[]{:S(2)}) collective-permute-start(bf16[1,34,384]{2,1,0:T(8,128)(2,1)S(1)} %get-tuple-element.104), channel_id=1, source_target_pairs={{1,0},{2,1},{3,2},{4,3},{5,4},{6,5},{7,6},{9,8},{10,9},{11,10},{12... | collective-permute-start | bytes 78344 | tf_op jit(solution)/shard_map/ppermute | solution.py:17
  82.6 1.1 reshape.98
  84.5 1.2 reshape.99
  86.8 3.5 %all-to-all-start = ((bf16[8,2,32,384]{3,2,1,0:T(8,128)(2,1)}), bf16[8,2,32,384]{3,2,1,0:T(8,128)(2,1)S(1)}, u32[]{:S(2)}, u32[]{:S(2)}) async-start(bf16[8,2,32,384]{3,2,1,0:T(8,128)(2,1)} %slice.679), calls=%async_computation | async-start | bytes 786432 | tf_op jit(solution)/shard_map/all_to_all | solution.py:85
  91.7 9.6 %all-to-all-done = bf16[8,2,32,384]{3,2,1,0:T(8,128)(2,1)S(1)} async-done(((bf16[8,2,32,384]{3,2,1,0:T(8,128)(2,1)}), bf16[8,2,32,384]{3,2,1,0:T(8,128)(2,1)S(1)}, u32[]{:S(2)}, u32[]{:S(2)}) %all-to-all-start) | async-done | bytes 393248 | tf_op jit(solution)/shard_map/all_to_all | solution.py:85
  101.4 5.3 %collective-permute-start.12 = (bf16[2,1,128,384]{3,2,1,0:T(8,128)(2,1)S(1)}, bf16[2,1,128,384]{3,2,1,0:T(8,128)(2,1)S(1)}, u32[]{:S(2)}, u32[]{:S(2)}) collective-permute-start(bf16[2,1,128,384]{3,2,1,0:T(8,128)(2,1)S(1)} %get-tuple-element.92), channel_id=1, source_target_pairs={{0,1},{1,2},{2,3},{3,4},{4,5},{5,6},{6,7},{8,9},{9,10},{10,11},{11... | collective-permute-start | bytes 589832 | tf_op jit(solution)/shard_map/ppermute | solution.py:16
  106.7 2.1 %collective-permute-start.13 = (bf16[2,1,128,384]{3,2,1,0:T(8,128)(2,1)S(1)}, bf16[2,1,128,384]{3,2,1,0:T(8,128)(2,1)S(1)}, u32[]{:S(2)}, u32[]{:S(2)}) collective-permute-start(bf16[2,1,128,384]{3,2,1,0:T(8,128)(2,1)S(1)} %get-tuple-element.93), channel_id=1, source_target_pairs={{1,0},{2,1},{3,2},{4,3},{5,4},{6,5},{7,6},{9,8},{10,9},{11,10},{12... | collective-permute-start | bytes 589832 | tf_op jit(solution)/shard_map/ppermute | solution.py:17
  109.8 3.8 %collective-permute-done.13 = bf16[2,1,128,384]{3,2,1,0:T(8,128)(2,1)S(1)} collective-permute-done((bf16[2,1,128,384]{3,2,1,0:T(8,128)(2,1)S(1)}, bf16[2,1,128,384]{3,2,1,0:T(8,128)(2,1)S(1)}, u32[]{:S(2)}, u32[]{:S(2)}) %collective-permute-start.13) | collective-permute-done | bytes 196640 | tf_op jit(solution)/shard_map/ppermute | solution.py:17
  116.8 7.8 %fusion.264 = (bf16[2,4,256,384]{3,1,2,0:T(4,128)(2,1)S(1)}, bf16[2,4,256,384]{3,1,2,0:T(4,128)(2,1)S(1)}, bf16[2,4,256,384]{3,1,2,0:T(4,128)(2,1)S(1)}, bf16[2,...) fusion(bf16[2,8,260,384]{3,1,2,0:T(8,128)(2,1)S(1)} %bitcast.142), kind=kLoop, calls=%fused_computation.243 | loop fusion | bytes 28311552 | tf_op jit(solution)/shard_map/slice | solution.py:35
  127.2 2.2 %fusion.6 = f32[2,4,256,192]{2,3,1,0:T(8,128)S(1)} fusion(bf16[2,4,256,384]{3,2,1,0:T(8,128)(2,1)S(1)} %copy.54, bf16[2,4,256,384]{3,2,1,0:T(8,128)(2,1)S(1)} %copy.53, bf16[2,4,256,384]{3,2,1,0:T(8,128)(2,1)S(1)} %copy.52, bf16[1152,192,1,1]{0,1,2,3:T(8,128)(2,1)S(1)} %copy-done.4), kind=kOutput, calls=%fused_computation.6 | convolution fusion | flops 920125440 | bytes 6733824 | tf_op jit(solution)/shard_map/...c,cd->...d/dot_general | solution.py:38
  129.5 2.3 %fusion = f32[2,4,256,192]{2,3,1,0:T(8,128)S(1)} fusion(bf16[2,4,256,384]{3,2,1,0:T(8,128)(2,1)S(1)} %copy.51, bf16[2,4,256,384]{3,2,1,0:T(8,128)(2,1)S(1)} %copy.50, bf16[2,4,256,384]{3,2,1,0:T(8,128)(2,1)S(1)} %copy.49, bf16[1152,192,1,1]{0,1,2,3:T(8,128)(2,1)S(1)} %copy-done.2), kind=kOutput, calls=%fused_computation | convolution fusion | flops 920125440 | bytes 6733824 | tf_op jit(solution)/shard_map/...c,cd->...d/dot_general | solution.py:38
  131.8 2.7 %add_convert_fusion = bf16[2,4,256,192]{2,3,1,0:T(8,128)(2,1)} fusion(f32[2,4,256,192]{2,3,1,0:T(8,128)S(1)} %fusion, f32[2,4,256,192]{2,3,1,0:T(8,128)S(1)} %fusion.6, bf16[2,4,256,384]{3,2,1,0:T(8,128)(2,1)S(1)} %copy.57, bf16[2,4,256,384]{3,2,1,0:T(8,128)(2,1)S(1)} %copy.56, bf16[2,4,256,384]{3,2,1,0:T(8,128)(2,1)S(1)} %copy.55, f32[192]{0:T(256)S(1)} %copy-done.8, ...), kind=kOutput, calls=%fused_computation.29 | convolution fusion | flops 921698304 | bytes 9093888 | tf_op jit(solution)/shard_map/...c,cd->...d/dot_general | solution.py:38
  (106 shorter events, 34.9 us)
Async XLA Ops:
  3.2 9.2 %collective-permute-start = (bf16[9,2,1,384]{3,2,1,0:T(2,128)(2,1)S(1)}, bf16[9,2,1,384]{3,2,1,0:T(2,128)(2,1)S(1)}, u32[]{:S(2)}, u32[]{:S(2)}) collective-permute-start(bf16[9,2,1,384]{3,2,1,0:T(2,128)(2,1)S(1)} %get-tuple-element.90), channel_id=1, source_target_pairs={{0,8},{8,16},{16,24},{1,9},{9,17},{17,25},{2,10},{10,18},{18,26},{... | collective-permute-start | bytes 41480 | tf_op jit(solution)/shard_map/ppermute | solution.py:16
  7.3 5.1 %collective-permute-start.1 = (bf16[9,2,1,384]{3,2,1,0:T(2,128)(2,1)S(1)}, bf16[9,2,1,384]{3,2,1,0:T(2,128)(2,1)S(1)}, u32[]{:S(2)}, u32[]{:S(2)}) collective-permute-start(bf16[9,2,1,384]{3,2,1,0:T(2,128)(2,1)S(1)} %get-tuple-element.91), channel_id=1, source_target_pairs={{8,0},{16,8},{24,16},{9,1},{17,9},{25,17},{10,2},{18,10},{26,18},{... | collective-permute-start | bytes 41480 | tf_op jit(solution)/shard_map/ppermute | solution.py:17
  12.8 8.0 %collective-permute-start.2 = (bf16[9,1,34,384]{3,2,1,0:T(8,128)(2,1)S(1)}, bf16[9,1,34,384]{3,2,1,0:T(8,128)(2,1)S(1)}, u32[]{:S(2)}, u32[]{:S(2)}) collective-permute-start(bf16[9,1,34,384]{3,2,1,0:T(8,128)(2,1)S(1)} %get-tuple-element.82), channel_id=1, source_target_pairs={{0,1},{1,2},{2,3},{3,4},{4,5},{5,6},{6,7},{8,9},{9,10},{10,11},{11... | collective-permute-start | bytes 705032 | tf_op jit(solution)/shard_map/ppermute | solution.py:16
  17.3 8.1 %collective-permute-start.3 = (bf16[9,1,34,384]{3,2,1,0:T(8,128)(2,1)S(1)}, bf16[9,1,34,384]{3,2,1,0:T(8,128)(2,1)S(1)}, u32[]{:S(2)}, u32[]{:S(2)}) collective-permute-start(bf16[9,1,34,384]{3,2,1,0:T(8,128)(2,1)S(1)} %get-tuple-element.83), channel_id=1, source_target_pairs={{1,0},{2,1},{3,2},{4,3},{5,4},{6,5},{7,6},{9,8},{10,9},{11,10},{12... | collective-permute-start | bytes 705032 | tf_op jit(solution)/shard_map/ppermute | solution.py:17
  33.9 7.5 %slice-start = ((s8[7962624]{0:T(1024)(128)(4,1)}), s8[4194304]{0:T(1024)(128)(4,1)S(1)}, s32[]{:S(2)}) async-start(s8[7962624]{0:T(1024)(128)(4,1)} %bitcast.143), calls=%async_computation.1 | async-start | bytes 8388608
  33.9 1.0 copy-start.6
  34.0 7.5 %slice-start.1 = ((s8[7962624]{0:T(1024)(128)(4,1)}), s8[3768320]{0:T(1024)(128)(4,1)S(1)}, s32[]{:S(2)}) async-start(s8[7962624]{0:T(1024)(128)(4,1)} %bitcast.143), calls=%async_computation.2 | async-start | bytes 7536640
  34.9 1.2 copy-start.5
  36.5 6.1 %collective-permute-start.4 = (bf16[9,2,1,384]{3,2,1,0:T(2,128)(2,1)S(1)}, bf16[9,2,1,384]{3,2,1,0:T(2,128)(2,1)S(1)}, u32[]{:S(2)}, u32[]{:S(2)}) collective-permute-start(bf16[9,2,1,384]{3,2,1,0:T(2,128)(2,1)S(1)} %get-tuple-element.88), channel_id=1, source_target_pairs={{0,8},{8,16},{16,24},{1,9},{9,17},{17,25},{2,10},{10,18},{18,26},{... | collective-permute-start | bytes 41480 | tf_op jit(solution)/shard_map/ppermute | solution.py:16
  40.2 4.6 %collective-permute-start.5 = (bf16[9,2,1,384]{3,2,1,0:T(2,128)(2,1)S(1)}, bf16[9,2,1,384]{3,2,1,0:T(2,128)(2,1)S(1)}, u32[]{:S(2)}, u32[]{:S(2)}) collective-permute-start(bf16[9,2,1,384]{3,2,1,0:T(2,128)(2,1)S(1)} %get-tuple-element.89), channel_id=1, source_target_pairs={{8,0},{16,8},{24,16},{9,1},{17,9},{25,17},{10,2},{18,10},{26,18},{... | collective-permute-start | bytes 41480 | tf_op jit(solution)/shard_map/ppermute | solution.py:17
  45.1 6.6 %collective-permute-start.6 = (bf16[9,1,34,384]{3,2,1,0:T(8,128)(2,1)S(1)}, bf16[9,1,34,384]{3,2,1,0:T(8,128)(2,1)S(1)}, u32[]{:S(2)}, u32[]{:S(2)}) collective-permute-start(bf16[9,1,34,384]{3,2,1,0:T(8,128)(2,1)S(1)} %get-tuple-element.80), channel_id=1, source_target_pairs={{0,1},{1,2},{2,3},{3,4},{4,5},{5,6},{6,7},{8,9},{9,10},{10,11},{11... | collective-permute-start | bytes 705032 | tf_op jit(solution)/shard_map/ppermute | solution.py:16
  48.3 8.7 %collective-permute-start.7 = (bf16[9,1,34,384]{3,2,1,0:T(8,128)(2,1)S(1)}, bf16[9,1,34,384]{3,2,1,0:T(8,128)(2,1)S(1)}, u32[]{:S(2)}, u32[]{:S(2)}) collective-permute-start(bf16[9,1,34,384]{3,2,1,0:T(8,128)(2,1)S(1)} %get-tuple-element.81), channel_id=1, source_target_pairs={{1,0},{2,1},{3,2},{4,3},{5,4},{6,5},{7,6},{9,8},{10,9},{11,10},{12... | collective-permute-start | bytes 705032 | tf_op jit(solution)/shard_map/ppermute | solution.py:17
  65.3 1.0 copy-start
  65.3 1.0 copy-start.7
  66.3 13.8 %copy-start.1 = (bf16[3,3,384,192]{2,3,1,0:T(8,128)(2,1)S(1)}, bf16[3,3,384,192]{2,3,1,0:T(8,128)(2,1)}, u32[]{:S(2)}) copy-start(bf16[3,3,384,192]{2,3,1,0:T(8,128)(2,1)} %param.16) | copy-start | bytes 3981316
  67.4 4.5 %collective-permute-start.8 = (bf16[2,1,384]{2,1,0:T(2,128)(2,1)S(1)}, bf16[2,1,384]{2,1,0:T(2,128)(2,1)S(1)}, u32[]{:S(2)}, u32[]{:S(2)}) collective-permute-start(bf16[2,1,384]{2,1,0:T(2,128)(2,1)S(1)} %get-tuple-element.105), channel_id=1, source_target_pairs={{0,8},{8,16},{16,24},{1,9},{9,17},{17,25},{2,10},{10,18},{18,26},{... | collective-permute-start | bytes 4616 | tf_op jit(solution)/shard_map/ppermute | solution.py:16
  70.6 4.3 %collective-permute-start.9 = (bf16[2,1,384]{2,1,0:T(2,128)(2,1)S(1)}, bf16[2,1,384]{2,1,0:T(2,128)(2,1)S(1)}, u32[]{:S(2)}, u32[]{:S(2)}) collective-permute-start(bf16[2,1,384]{2,1,0:T(2,128)(2,1)S(1)} %get-tuple-element.106), channel_id=1, source_target_pairs={{8,0},{16,8},{24,16},{9,1},{17,9},{25,17},{10,2},{18,10},{26,18},{... | collective-permute-start | bytes 4616 | tf_op jit(solution)/shard_map/ppermute | solution.py:17
  75.0 15.3 %collective-permute-start.10 = (bf16[1,34,384]{2,1,0:T(8,128)(2,1)S(1)}, bf16[1,34,384]{2,1,0:T(8,128)(2,1)S(1)}, u32[]{:S(2)}, u32[]{:S(2)}) collective-permute-start(bf16[1,34,384]{2,1,0:T(8,128)(2,1)S(1)} %get-tuple-element.103), channel_id=1, source_target_pairs={{0,1},{1,2},{2,3},{3,4},{4,5},{5,6},{6,7},{8,9},{9,10},{10,11},{11... | collective-permute-start | bytes 78344 | tf_op jit(solution)/shard_map/ppermute | solution.py:16
  78.2 12.1 %collective-permute-start.11 = (bf16[1,34,384]{2,1,0:T(8,128)(2,1)S(1)}, bf16[1,34,384]{2,1,0:T(8,128)(2,1)S(1)}, u32[]{:S(2)}, u32[]{:S(2)}) collective-permute-start(bf16[1,34,384]{2,1,0:T(8,128)(2,1)S(1)} %get-tuple-element.104), channel_id=1, source_target_pairs={{1,0},{2,1},{3,2},{4,3},{5,4},{6,5},{7,6},{9,8},{10,9},{11,10},{12... | collective-permute-start | bytes 78344 | tf_op jit(solution)/shard_map/ppermute | solution.py:17
  86.8 14.4 %all-to-all-start = ((bf16[8,2,32,384]{3,2,1,0:T(8,128)(2,1)}), bf16[8,2,32,384]{3,2,1,0:T(8,128)(2,1)S(1)}, u32[]{:S(2)}, u32[]{:S(2)}) async-start(bf16[8,2,32,384]{3,2,1,0:T(8,128)(2,1)} %slice.679), calls=%async_computation | async-start | bytes 786432 | tf_op jit(solution)/shard_map/all_to_all | solution.py:85
  91.3 17.5 %copy-start.8 = (f32[192]{0:T(256)S(1)}, f32[192]{0:T(256)}, u32[]{:S(2)}) copy-start(f32[192]{0:T(256)} %param.17) | copy-start | bytes 2308
  101.4 8.5 %collective-permute-start.12 = (bf16[2,1,128,384]{3,2,1,0:T(8,128)(2,1)S(1)}, bf16[2,1,128,384]{3,2,1,0:T(8,128)(2,1)S(1)}, u32[]{:S(2)}, u32[]{:S(2)}) collective-permute-start(bf16[2,1,128,384]{3,2,1,0:T(8,128)(2,1)S(1)} %get-tuple-element.92), channel_id=1, source_target_pairs={{0,1},{1,2},{2,3},{3,4},{4,5},{5,6},{6,7},{8,9},{9,10},{10,11},{11... | collective-permute-start | bytes 589832 | tf_op jit(solution)/shard_map/ppermute | solution.py:16
  106.7 7.0 %collective-permute-start.13 = (bf16[2,1,128,384]{3,2,1,0:T(8,128)(2,1)S(1)}, bf16[2,1,128,384]{3,2,1,0:T(8,128)(2,1)S(1)}, u32[]{:S(2)}, u32[]{:S(2)}) collective-permute-start(bf16[2,1,128,384]{3,2,1,0:T(8,128)(2,1)S(1)} %get-tuple-element.93), channel_id=1, source_target_pairs={{1,0},{2,1},{3,2},{4,3},{5,4},{6,5},{7,6},{9,8},{10,9},{11,10},{12... | collective-permute-start | bytes 589832 | tf_op jit(solution)/shard_map/ppermute | solution.py:17
  126.2 1.0 copy-start.4
  127.2 2.2 %copy-start.2 = (bf16[1152,192,1,1]{0,1,2,3:T(8,128)(2,1)S(1)}, bf16[1152,192,1,1]{0,1,2,3:T(8,128)(2,1)}, u32[]{:S(2)}) copy-start(bf16[1152,192,1,1]{0,1,2,3:T(8,128)(2,1)} %reshape.97) | copy-start | bytes 1327108
  129.5 2.3 %copy-start.3 = (bf16[1152,192,1,1]{0,1,2,3:T(8,128)(2,1)S(1)}, bf16[1152,192,1,1]{0,1,2,3:T(8,128)(2,1)}, u32[]{:S(2)}) copy-start(bf16[1152,192,1,1]{0,1,2,3:T(8,128)(2,1)} %reshape.99) | copy-start | bytes 1327108
where the time goes:
time: 135 us; the launch traced here: 134 us
  starting transfers between devices  42.5 us (31%)
  local copies, waits for them, and re-layouts  30.6 us (23%)
  waiting for transfers between devices  29.6 us (22%)
  matrix products  25.2 us (19%)
  other arithmetic  5.07 us (4%)
  between operations  1.5 us (1%)
    ppermute x7, starting transfers between devices, with_halo(): before = lax.ppermute(last, axis, up)  27.1 us
    dot_general x24, matrix products, row_taps(): jnp.einsum('...c,cd->...d', widened, merged, preferred_element_type=jnp.f...  25.2 us
    ppermute x7, waiting for transfers between devices, with_halo(): after = lax.ppermute(leading, axis, down)  18.9 us
    slice x7, local copies, waits for them, and re-layouts, row_taps(): slab_rows[..., offset:offset + col_count, :]  12.7 us
    ppermute x7, starting transfers between devices, with_halo(): after = lax.ppermute(leading, axis, down)  12 us
    all_to_all x1, waiting for transfers between devices, body(): lax.all_to_all(summed[1:], 'tm', split_axis=0, concat_axis=2, tiled=True)  9.57 us
    slice x3, local copies, waits for them, and re-layouts, plane_conv(): summed = row_taps(padded[..., 0:row_count, :, :], tap_weights[0])  5.34 us
    another operation x6, local copies, waits for them, and re-layouts, row_taps(): merged = tap_weights.reshape(3 * tap_weights.shape[1], tap_weights.shape[2])  4.56 us
  transfers between devices with their start and end apart: 15, of which 8 were waited for; matrix products, arithmetic and copies ran while one was open for 12% of the time, Pallas kernels for 0%

commit v1 on v0

--- a/solution.py
+++ b/solution.py
@@ -82,7 +82,10 @@
     first_image = (enlarge_conv(first_rimmed, up_weight, 0, 2 * quarter) + up_bias).astype(
         jnp.bfloat16
     )
-    later_block = lax.all_to_all(summed[1:], "tm", split_axis=0, concat_axis=2, tiled=True)
+    later_block = jnp.concatenate(
+        lax.all_to_all(jnp.stack(jnp.split(summed[1:], lax.axis_size("tm"), axis=0)), "tm", 0, 0),
+        axis=2,
+    )
     later_in = column_pad(with_halo(later_block, (("height", 1),), 1))
     later_images = (enlarge_conv(later_in, up_weight, 0, 2 * width_all) + up_bias).astype(
         jnp.bfloat16

time: 135 us -> 141 us (1.044)
  local copies, waits for them, and re-layouts: 30.6 us -> 37.4 us
  waiting for transfers between devices: 29.6 us -> 26.7 us
    unnamed x32 -> x52, local copies, waits for them, and re-layouts: 3.37 us -> 6.72 us
    slice x3, local copies, waits for them, and re-layouts: 5.34 us -> 7.84 us  [plane_conv(): summed = row_taps(padded[..., 0:row_count, :, :], tap_weights[0])]
    ppermute x7, waiting for transfers between devices: 18.9 us -> 16.7 us  [with_halo(): after = lax.ppermute(leading, axis, down)]
    another operation x6, local copies, waits for them, and re-layouts: 4.56 us -> 6.24 us  [row_taps(): merged = tap_weights.reshape(3 * tap_weights.shape[1], tap_weights.shape[2])]
  transfers between devices with their start and end apart: 15 -> 15, of which waited for: 8 -> 7; matrix products, arithmetic and copies ran while one was open for 12% -> 14% of each run, Pallas kernels for 0% -> 0%
where the time goes in v1:
time: 141 us; the launch traced here: 140 us
  starting transfers between devices  43 us (30%)
  local copies, waits for them, and re-layouts  37.4 us (27%)
  waiting for transfers between devices  26.7 us (19%)
  matrix products  25.1 us (18%)
  other arithmetic  6.05 us (4%)
  between operations  1.51 us (1%)
    ppermute x7, starting transfers between devices, with_halo(): before = lax.ppermute(last, axis, up)  26.8 us
    dot_general x24, matrix products, row_taps(): jnp.einsum('...c,cd->...d', widened, merged, preferred_element_type=jnp.f...  25.1 us
    ppermute x7, waiting for transfers between devices, with_halo(): after = lax.ppermute(leading, axis, down)  16.7 us
    slice x7, local copies, waits for them, and re-layouts, row_taps(): slab_rows[..., offset:offset + col_count, :]  12.7 us
    ppermute x7, starting transfers between devices, with_halo(): after = lax.ppermute(leading, axis, down)  12.6 us
    all_to_all x1, waiting for transfers between devices, body(): lax.all_to_all(jnp.stack(jnp.split(summed[1:], lax.axis_size('tm'), axis=...  9.13 us
    slice x3, local copies, waits for them, and re-layouts, plane_conv(): summed = row_taps(padded[..., 0:row_count, :, :], tap_weights[0])  7.84 us
    unnamed x52, local copies, waits for them, and re-layouts  6.72 us
  transfers between devices with their start and end apart: 15, of which 7 were waited for; matrix products, arithmetic and copies ran while one was open for 14% of the time, Pallas kernels for 0%

profile of v1, /device:TPU:1, one launch (start us, length us, event | category | flops | bytes accessed | tf_op | source)
XLA Modules:
  0.0 139.7 jit_solution(702861016025706970)
XLA Ops:
  0.6 1.2 fusion.211
  1.8 1.5 %fusion.218 = bf16[9,2,32,384]{3,2,1,0:T(8,128)(2,1)S(1)} fusion(bf16[9,2,32,384]{3,2,1,0:T(8,128)(2,1)} %param.9, f32[384]{0:T(512)} %param.10, f32[9,2,32]{2,1,0:T(2,128)S(1)} %add_rsqrt_fusion.1), kind=kLoop, calls=%fused_computation.183 | loop fusion | flops 1769472 | bytes 888576 | tf_op jit(solution)/shard_map/convert_element_type | solution.py:76
  3.4 4.0 %collective-permute-start = (bf16[9,2,1,384]{3,2,1,0:T(2,128)(2,1)S(1)}, bf16[9,2,1,384]{3,2,1,0:T(2,128)(2,1)S(1)}, u32[]{:S(2)}, u32[]{:S(2)}) collective-permute-start(bf16[9,2,1,384]{3,2,1,0:T(2,128)(2,1)S(1)} %get-tuple-element.94), channel_id=1, source_target_pairs={{0,8},{8,16},{16,24},{1,9},{9,17},{17,25},{2,10},{10,18},{18,26},{... | collective-permute-start | bytes 41480 | tf_op jit(solution)/shard_map/ppermute | solution.py:16
  7.5 1.6 %collective-permute-start.1 = (bf16[9,2,1,384]{3,2,1,0:T(2,128)(2,1)S(1)}, bf16[9,2,1,384]{3,2,1,0:T(2,128)(2,1)S(1)}, u32[]{:S(2)}, u32[]{:S(2)}) collective-permute-start(bf16[9,2,1,384]{3,2,1,0:T(2,128)(2,1)S(1)} %get-tuple-element.95), channel_id=1, source_target_pairs={{8,0},{16,8},{24,16},{9,1},{17,9},{25,17},{10,2},{18,10},{26,18},{... | collective-permute-start | bytes 41480 | tf_op jit(solution)/shard_map/ppermute | solution.py:17
  9.0 4.0 %fusion.263 = (bf16[1,1,3,384,384]{4,3,2,1,0:T(8,128)(2,1)S(1)}, bf16[1,1,3,384,384]{4,3,2,1,0:T(8,128)(2,1)S(1)}, bf16[1,1,3,384,384]{4,3,2,1,0:T(8,128)(2,1)S(...) fusion(bf16[3,3,3,384,384]{4,3,2,1,0:T(8,128)(2,1)} %param.11), kind=kLoop, calls=%fused_computation.247 | loop fusion | bytes 15925248 | tf_op jit(solution)/shard_map/slice | solution.py:43
  13.1 3.5 %fusion.262 = (bf16[1,1,3,384,384]{4,3,2,1,0:T(8,128)(2,1)S(1)}, bf16[1,1,3,384,384]{4,3,2,1,0:T(8,128)(2,1)}, bf16[1,1,3,384,384]{4,3,2,1,0:T(8,128)(2,1)}, bf1...) fusion(bf16[3,3,3,384,384]{4,3,2,1,0:T(8,128)(2,1)S(1)} %bitcas, ...), kind=kLoop, calls=%fused_computation.246 | loop fusion | bytes 15925248 | tf_op jit(solution)/shard_map/slice | solution.py:43
  16.9 4.0 %collective-permute-start.2 = (bf16[9,1,34,384]{3,2,1,0:T(8,128)(2,1)S(1)}, bf16[9,1,34,384]{3,2,1,0:T(8,128)(2,1)S(1)}, u32[]{:S(2)}, u32[]{:S(2)}) collective-permute-start(bf16[9,1,34,384]{3,2,1,0:T(8,128)(2,1)S(1)} %get-tuple-element.82), channel_id=1, source_target_pairs={{0,1},{1,2},{2,3},{3,4},{4,5},{5,6},{6,7},{8,9},{9,10},{10,11},{11... | collective-permute-start | bytes 705032 | tf_op jit(solution)/shard_map/ppermute | solution.py:16
  20.8 1.9 %collective-permute-start.3 = (bf16[9,1,34,384]{3,2,1,0:T(8,128)(2,1)S(1)}, bf16[9,1,34,384]{3,2,1,0:T(8,128)(2,1)S(1)}, u32[]{:S(2)}, u32[]{:S(2)}) collective-permute-start(bf16[9,1,34,384]{3,2,1,0:T(8,128)(2,1)S(1)} %get-tuple-element.83), channel_id=1, source_target_pairs={{1,0},{2,1},{3,2},{4,3},{5,4},{6,5},{7,6},{9,8},{10,9},{11,10},{12... | collective-permute-start | bytes 705032 | tf_op jit(solution)/shard_map/ppermute | solution.py:17
  24.3 4.6 %collective-permute-done.3 = bf16[9,1,34,384]{3,2,1,0:T(8,128)(2,1)S(1)} collective-permute-done((bf16[9,1,34,384]{3,2,1,0:T(8,128)(2,1)S(1)}, bf16[9,1,34,384]{3,2,1,0:T(8,128)(2,1)S(1)}, u32[]{:S(2)}, u32[]{:S(2)}) %collective-permute-start.3) | collective-permute-done | bytes 235040 | tf_op jit(solution)/shard_map/ppermute | solution.py:17
  29.2 1.7 %fusion.266 = (bf16[9,2,32,384]{3,2,1,0:T(8,128)(2,1)S(1)}, bf16[9,2,32,384]{3,2,1,0:T(8,128)(2,1)S(1)}, bf16[9,2,32,384]{3,2,1,0:T(8,128)(2,1)S(1)}, bf16[9,2,3...) fusion(bf16[11,4,34,384]{3,2,1,0:T(8,128)(2,1)S(1)} %fusion.33), kind=kLoop, calls=%fused_computation.250 | loop fusion | bytes 15925248 | tf_op jit(solution)/shard_map/slice | solution.py:35
  39.8 4.3 %collective-permute-start.4 = (bf16[9,2,1,384]{3,2,1,0:T(2,128)(2,1)S(1)}, bf16[9,2,1,384]{3,2,1,0:T(2,128)(2,1)S(1)}, u32[]{:S(2)}, u32[]{:S(2)}) collective-permute-start(bf16[9,2,1,384]{3,2,1,0:T(2,128)(2,1)S(1)} %get-tuple-element.92), channel_id=1, source_target_pairs={{0,8},{8,16},{16,24},{1,9},{9,17},{17,25},{2,10},{10,18},{18,26},{... | collective-permute-start | bytes 41480 | tf_op jit(solution)/shard_map/ppermute | solution.py:16
  44.1 1.5 %collective-permute-start.5 = (bf16[9,2,1,384]{3,2,1,0:T(2,128)(2,1)S(1)}, bf16[9,2,1,384]{3,2,1,0:T(2,128)(2,1)S(1)}, u32[]{:S(2)}, u32[]{:S(2)}) collective-permute-start(bf16[9,2,1,384]{3,2,1,0:T(2,128)(2,1)S(1)} %get-tuple-element.93), channel_id=1, source_target_pairs={{8,0},{16,8},{24,16},{9,1},{17,9},{25,17},{10,2},{18,10},{26,18},{... | collective-permute-start | bytes 41480 | tf_op jit(solution)/shard_map/ppermute | solution.py:17
  48.8 1.2 reshape.106
  51.5 1.2 reshape.107
  53.5 2.0 %collective-permute-start.6 = (bf16[9,1,34,384]{3,2,1,0:T(8,128)(2,1)S(1)}, bf16[9,1,34,384]{3,2,1,0:T(8,128)(2,1)S(1)}, u32[]{:S(2)}, u32[]{:S(2)}) collective-permute-start(bf16[9,1,34,384]{3,2,1,0:T(8,128)(2,1)S(1)} %get-tuple-element.80), channel_id=1, source_target_pairs={{0,1},{1,2},{2,3},{3,4},{4,5},{5,6},{6,7},{8,9},{9,10},{10,11},{11... | collective-permute-start | bytes 705032 | tf_op jit(solution)/shard_map/ppermute | solution.py:16
  55.5 2.3 %collective-permute-start.7 = (bf16[9,1,34,384]{3,2,1,0:T(8,128)(2,1)S(1)}, bf16[9,1,34,384]{3,2,1,0:T(8,128)(2,1)S(1)}, u32[]{:S(2)}, u32[]{:S(2)}) collective-permute-start(bf16[9,1,34,384]{3,2,1,0:T(8,128)(2,1)S(1)} %get-tuple-element.81), channel_id=1, source_target_pairs={{1,0},{2,1},{3,2},{4,3},{5,4},{6,5},{7,6},{9,8},{10,9},{11,10},{12... | collective-permute-start | bytes 705032 | tf_op jit(solution)/shard_map/ppermute | solution.py:17
  59.0 5.3 %collective-permute-done.7 = bf16[9,1,34,384]{3,2,1,0:T(8,128)(2,1)S(1)} collective-permute-done((bf16[9,1,34,384]{3,2,1,0:T(8,128)(2,1)S(1)}, bf16[9,1,34,384]{3,2,1,0:T(8,128)(2,1)S(1)}, u32[]{:S(2)}, u32[]{:S(2)}) %collective-permute-start.7) | collective-permute-done | bytes 235040 | tf_op jit(solution)/shard_map/ppermute | solution.py:17
  64.6 1.8 %fusion.265 = (bf16[9,2,32,384]{3,2,1,0:T(8,128)(2,1)S(1)}, bf16[9,2,32,384]{3,2,1,0:T(8,128)(2,1)S(1)}, bf16[9,2,32,384]{3,2,1,0:T(8,128)(2,1)S(1)}, bf16[9,2,3...) fusion(bf16[11,4,34,384]{3,2,1,0:T(8,128)(2,1)S(1)} %fusion.31), kind=kLoop, calls=%fused_computation.249 | loop fusion | bytes 15925248 | tf_op jit(solution)/shard_map/slice | solution.py:35
  77.3 4.3 %collective-permute-start.8 = (bf16[2,1,384]{2,1,0:T(2,128)(2,1)S(1)}, bf16[2,1,384]{2,1,0:T(2,128)(2,1)S(1)}, u32[]{:S(2)}, u32[]{:S(2)}) collective-permute-start(bf16[2,1,384]{2,1,0:T(2,128)(2,1)S(1)} %get-tuple-element.109), channel_id=1, source_target_pairs={{0,8},{8,16},{16,24},{1,9},{9,17},{17,25},{2,10},{10,18},{18,26},{... | collective-permute-start | bytes 4616 | tf_op jit(solution)/shard_map/ppermute | solution.py:16
  81.6 1.3 collective-permute-start.9
  83.0 3.0 %collective-permute-done.9 = bf16[2,1,384]{2,1,0:T(2,128)(2,1)S(1)} collective-permute-done((bf16[2,1,384]{2,1,0:T(2,128)(2,1)S(1)}, bf16[2,1,384]{2,1,0:T(2,128)(2,1)S(1)}, u32[]{:S(2)}, u32[]{:S(2)}) %collective-permute-start.9) | collective-permute-done | bytes 1568 | tf_op jit(solution)/shard_map/ppermute | solution.py:17
  86.0 3.2 %collective-permute-start.10 = (bf16[1,34,384]{2,1,0:T(8,128)(2,1)S(1)}, bf16[1,34,384]{2,1,0:T(8,128)(2,1)S(1)}, u32[]{:S(2)}, u32[]{:S(2)}) collective-permute-start(bf16[1,34,384]{2,1,0:T(8,128)(2,1)S(1)} %get-tuple-element.107), channel_id=1, source_target_pairs={{0,1},{1,2},{2,3},{3,4},{4,5},{5,6},{6,7},{8,9},{9,10},{10,11},{11... | collective-permute-start | bytes 78344 | tf_op jit(solution)/shard_map/ppermute | solution.py:16
  89.2 1.9 %collective-permute-start.11 = (bf16[1,34,384]{2,1,0:T(8,128)(2,1)S(1)}, bf16[1,34,384]{2,1,0:T(8,128)(2,1)S(1)}, u32[]{:S(2)}, u32[]{:S(2)}) collective-permute-start(bf16[1,34,384]{2,1,0:T(8,128)(2,1)S(1)} %get-tuple-element.108), channel_id=1, source_target_pairs={{1,0},{2,1},{3,2},{4,3},{5,4},{6,5},{7,6},{9,8},{10,9},{11,10},{12... | collective-permute-start | bytes 78344 | tf_op jit(solution)/shard_map/ppermute | solution.py:17
  91.9 3.6 %all-to-all-start = ((bf16[4,2,2,32,384]{4,3,2,1,0:T(8,128)(2,1)}), bf16[4,2,2,32,384]{4,3,2,1,0:T(8,128)(2,1)S(1)}, u32[]{:S(2)}, u32[]{:S(2)}) async-start(bf16[4,2,2,32,384]{4,3,2,1,0:T(8,128)(2,1)} %pad_maximum_fusion.9), calls=%async_computation | async-start | bytes 786432 | tf_op jit(solution)/shard_map/all_to_all | solution.py:86
  97.7 9.1 %all-to-all-done = bf16[4,2,2,32,384]{4,3,2,1,0:T(8,128)(2,1)S(1)} async-done(((bf16[4,2,2,32,384]{4,3,2,1,0:T(8,128)(2,1)}), bf16[4,2,2,32,384]{4,3,2,1,0:T(8,128)(2,1)S(1)}, u32[]{:S(2)}, u32[]{:S(2)}) %all-to-all-start) | async-done | bytes 393248 | tf_op jit(solution)/shard_map/all_to_all | solution.py:86
  106.9 5.0 %collective-permute-start.12 = (bf16[2,1,128,384]{3,2,1,0:T(8,128)(2,1)S(1)}, bf16[2,1,128,384]{3,2,1,0:T(8,128)(2,1)S(1)}, u32[]{:S(2)}, u32[]{:S(2)}) collective-permute-start(bf16[2,1,128,384]{3,2,1,0:T(8,128)(2,1)S(1)} %get-tuple-element.96), channel_id=1, source_target_pairs={{0,1},{1,2},{2,3},{3,4},{4,5},{5,6},{6,7},{8,9},{9,10},{10,11},{11... | collective-permute-start | bytes 589832 | tf_op jit(solution)/shard_map/ppermute | solution.py:16
  112.0 2.1 %collective-permute-start.13 = (bf16[2,1,128,384]{3,2,1,0:T(8,128)(2,1)S(1)}, bf16[2,1,128,384]{3,2,1,0:T(8,128)(2,1)S(1)}, u32[]{:S(2)}, u32[]{:S(2)}) collective-permute-start(bf16[2,1,128,384]{3,2,1,0:T(8,128)(2,1)S(1)} %get-tuple-element.97), channel_id=1, source_target_pairs={{1,0},{2,1},{3,2},{4,3},{5,4},{6,5},{7,6},{9,8},{10,9},{11,10},{12... | collective-permute-start | bytes 589832 | tf_op jit(solution)/shard_map/ppermute | solution.py:17
  115.1 3.8 %collective-permute-done.13 = bf16[2,1,128,384]{3,2,1,0:T(8,128)(2,1)S(1)} collective-permute-done((bf16[2,1,128,384]{3,2,1,0:T(8,128)(2,1)S(1)}, bf16[2,1,128,384]{3,2,1,0:T(8,128)(2,1)S(1)}, u32[]{:S(2)}, u32[]{:S(2)}) %collective-permute-start.13) | collective-permute-done | bytes 196640 | tf_op jit(solution)/shard_map/ppermute | solution.py:17
  122.0 7.8 %fusion.264 = (bf16[2,4,256,384]{3,1,2,0:T(4,128)(2,1)S(1)}, bf16[2,4,256,384]{3,1,2,0:T(4,128)(2,1)S(1)}, bf16[2,4,256,384]{3,1,2,0:T(4,128)(2,1)S(1)}, bf16[2,...) fusion(bf16[2,8,260,384]{3,1,2,0:T(8,128)(2,1)S(1)} %bitcast.148), kind=kLoop, calls=%fused_computation.248 | loop fusion | bytes 28311552 | tf_op jit(solution)/shard_map/slice | solution.py:35
  132.5 2.2 %fusion.6 = f32[2,4,256,192]{2,3,1,0:T(8,128)S(1)} fusion(bf16[2,4,256,384]{3,2,1,0:T(8,128)(2,1)S(1)} %copy.54, bf16[2,4,256,384]{3,2,1,0:T(8,128)(2,1)S(1)} %copy.53, bf16[2,4,256,384]{3,2,1,0:T(8,128)(2,1)S(1)} %copy.52, bf16[1152,192,1,1]{0,1,2,3:T(8,128)(2,1)S(1)} %copy-done.12), kind=kOutput, calls=%fused_computation.6 | convolution fusion | flops 920125440 | bytes 6733824 | tf_op jit(solution)/shard_map/...c,cd->...d/dot_general | solution.py:38
  134.8 2.3 %fusion = f32[2,4,256,192]{2,3,1,0:T(8,128)S(1)} fusion(bf16[2,4,256,384]{3,2,1,0:T(8,128)(2,1)S(1)} %copy.51, bf16[2,4,256,384]{3,2,1,0:T(8,128)(2,1)S(1)} %copy.50, bf16[2,4,256,384]{3,2,1,0:T(8,128)(2,1)S(1)} %copy.49, bf16[1152,192,1,1]{0,1,2,3:T(8,128)(2,1)S(1)} %copy-done.10), kind=kOutput, calls=%fused_computation | convolution fusion | flops 920125440 | bytes 6733824 | tf_op jit(solution)/shard_map/...c,cd->...d/dot_general | solution.py:38
  137.0 2.7 %add_convert_fusion = bf16[2,4,256,192]{2,3,1,0:T(8,128)(2,1)} fusion(f32[2,4,256,192]{2,3,1,0:T(8,128)S(1)} %fusion, f32[2,4,256,192]{2,3,1,0:T(8,128)S(1)} %fusion.6, bf16[2,4,256,384]{3,2,1,0:T(8,128)(2,1)S(1)} %copy.57, bf16[2,4,256,384]{3,2,1,0:T(8,128)(2,1)S(1)} %copy.56, bf16[2,4,256,384]{3,2,1,0:T(8,128)(2,1)S(1)} %copy.55, f32[192]{0:T(256)S(1)} %copy-done.18, ...), kind=kOutput, calls=%fused_computation.29 | convolution fusion | flops 921698304 | bytes 9093888 | tf_op jit(solution)/shard_map/...c,cd->...d/dot_general | solution.py:38
  (127 shorter events, 38.5 us)
Async XLA Ops:
  1.8 11.2 %slice-start = ((s8[7962624]{0:T(1024)(128)(4,1)}), s8[4194304]{0:T(1024)(128)(4,1)S(1)}, s32[]{:S(2)}) async-start(s8[7962624]{0:T(1024)(128)(4,1)} %bitcast.149), calls=%async_computation.1 | async-start | bytes 8388608
  3.4 13.1 %collective-permute-start = (bf16[9,2,1,384]{3,2,1,0:T(2,128)(2,1)S(1)}, bf16[9,2,1,384]{3,2,1,0:T(2,128)(2,1)S(1)}, u32[]{:S(2)}, u32[]{:S(2)}) collective-permute-start(bf16[9,2,1,384]{3,2,1,0:T(2,128)(2,1)S(1)} %get-tuple-element.94), channel_id=1, source_target_pairs={{0,8},{8,16},{16,24},{1,9},{9,17},{17,25},{2,10},{10,18},{18,26},{... | collective-permute-start | bytes 41480 | tf_op jit(solution)/shard_map/ppermute | solution.py:16
  7.4 5.6 %slice-start.1 = ((s8[7962624]{0:T(1024)(128)(4,1)}), s8[3768320]{0:T(1024)(128)(4,1)S(1)}, s32[]{:S(2)}) async-start(s8[7962624]{0:T(1024)(128)(4,1)} %bitcast.149), calls=%async_computation.2 | async-start | bytes 7536640
  7.5 9.1 %collective-permute-start.1 = (bf16[9,2,1,384]{3,2,1,0:T(2,128)(2,1)S(1)}, bf16[9,2,1,384]{3,2,1,0:T(2,128)(2,1)S(1)}, u32[]{:S(2)}, u32[]{:S(2)}) collective-permute-start(bf16[9,2,1,384]{3,2,1,0:T(2,128)(2,1)S(1)} %get-tuple-element.95), channel_id=1, source_target_pairs={{8,0},{16,8},{24,16},{9,1},{17,9},{25,17},{10,2},{18,10},{26,18},{... | collective-permute-start | bytes 41480 | tf_op jit(solution)/shard_map/ppermute | solution.py:17
  16.9 7.4 %collective-permute-start.2 = (bf16[9,1,34,384]{3,2,1,0:T(8,128)(2,1)S(1)}, bf16[9,1,34,384]{3,2,1,0:T(8,128)(2,1)S(1)}, u32[]{:S(2)}, u32[]{:S(2)}) collective-permute-start(bf16[9,1,34,384]{3,2,1,0:T(8,128)(2,1)S(1)} %get-tuple-element.82), channel_id=1, source_target_pairs={{0,1},{1,2},{2,3},{3,4},{4,5},{5,6},{6,7},{8,9},{9,10},{10,11},{11... | collective-permute-start | bytes 705032 | tf_op jit(solution)/shard_map/ppermute | solution.py:16
  20.8 8.1 %collective-permute-start.3 = (bf16[9,1,34,384]{3,2,1,0:T(8,128)(2,1)S(1)}, bf16[9,1,34,384]{3,2,1,0:T(8,128)(2,1)S(1)}, u32[]{:S(2)}, u32[]{:S(2)}) collective-permute-start(bf16[9,1,34,384]{3,2,1,0:T(8,128)(2,1)S(1)} %get-tuple-element.83), channel_id=1, source_target_pairs={{1,0},{2,1},{3,2},{4,3},{5,4},{6,5},{7,6},{9,8},{10,9},{11,10},{12... | collective-permute-start | bytes 705032 | tf_op jit(solution)/shard_map/ppermute | solution.py:17
  38.2 1.2 copy-start.15
  39.4 6.2 %copy-start.1 = (bf16[3,3,384,192]{2,3,1,0:T(8,128)(2,1)S(1)}, bf16[3,3,384,192]{2,3,1,0:T(8,128)(2,1)}, u32[]{:S(2)}) copy-start(bf16[3,3,384,192]{2,3,1,0:T(8,128)(2,1)} %param.16) | copy-start | bytes 3981316
  39.8 13.3 %collective-permute-start.4 = (bf16[9,2,1,384]{3,2,1,0:T(2,128)(2,1)S(1)}, bf16[9,2,1,384]{3,2,1,0:T(2,128)(2,1)S(1)}, u32[]{:S(2)}, u32[]{:S(2)}) collective-permute-start(bf16[9,2,1,384]{3,2,1,0:T(2,128)(2,1)S(1)} %get-tuple-element.92), channel_id=1, source_target_pairs={{0,8},{8,16},{16,24},{1,9},{9,17},{17,25},{2,10},{10,18},{18,26},{... | collective-permute-start | bytes 41480 | tf_op jit(solution)/shard_map/ppermute | solution.py:16
  44.1 9.1 %collective-permute-start.5 = (bf16[9,2,1,384]{3,2,1,0:T(2,128)(2,1)S(1)}, bf16[9,2,1,384]{3,2,1,0:T(2,128)(2,1)S(1)}, u32[]{:S(2)}, u32[]{:S(2)}) collective-permute-start(bf16[9,2,1,384]{3,2,1,0:T(2,128)(2,1)S(1)} %get-tuple-element.93), channel_id=1, source_target_pairs={{8,0},{16,8},{24,16},{9,1},{17,9},{25,17},{10,2},{18,10},{26,18},{... | collective-permute-start | bytes 41480 | tf_op jit(solution)/shard_map/ppermute | solution.py:17
  52.7 5.1 %copy-start.9 = (bf16[1,1,3,384,384]{4,3,2,1,0:T(8,128)(2,1)S(1)}, bf16[1,1,3,384,384]{4,3,2,1,0:T(8,128)(2,1)}, u32[]{:S(2)}) copy-start(bf16[1,1,3,384,384]{4,3,2,1,0:T(8,128)(2,1)} %get-tuple-element.10) | copy-start | bytes 2654212
  53.5 5.5 %collective-permute-start.6 = (bf16[9,1,34,384]{3,2,1,0:T(8,128)(2,1)S(1)}, bf16[9,1,34,384]{3,2,1,0:T(8,128)(2,1)S(1)}, u32[]{:S(2)}, u32[]{:S(2)}) collective-permute-start(bf16[9,1,34,384]{3,2,1,0:T(8,128)(2,1)S(1)} %get-tuple-element.80), channel_id=1, source_target_pairs={{0,1},{1,2},{2,3},{3,4},{4,5},{5,6},{6,7},{8,9},{9,10},{10,11},{11... | collective-permute-start | bytes 705032 | tf_op jit(solution)/shard_map/ppermute | solution.py:16
  55.5 8.7 %collective-permute-start.7 = (bf16[9,1,34,384]{3,2,1,0:T(8,128)(2,1)S(1)}, bf16[9,1,34,384]{3,2,1,0:T(8,128)(2,1)S(1)}, u32[]{:S(2)}, u32[]{:S(2)}) collective-permute-start(bf16[9,1,34,384]{3,2,1,0:T(8,128)(2,1)S(1)} %get-tuple-element.81), channel_id=1, source_target_pairs={{1,0},{2,1},{3,2},{4,3},{5,4},{6,5},{7,6},{9,8},{10,9},{11,10},{12... | collective-permute-start | bytes 705032 | tf_op jit(solution)/shard_map/ppermute | solution.py:17
  67.1 1.2 copy-start.8
  68.3 1.2 copy-start.7
  69.4 1.2 copy-start.6
  70.6 1.2 copy-start.5
  71.8 1.2 copy-start.4
  72.9 1.2 copy-start.3
  74.1 1.2 copy-start.2
  77.3 5.6 %collective-permute-start.8 = (bf16[2,1,384]{2,1,0:T(2,128)(2,1)S(1)}, bf16[2,1,384]{2,1,0:T(2,128)(2,1)S(1)}, u32[]{:S(2)}, u32[]{:S(2)}) collective-permute-start(bf16[2,1,384]{2,1,0:T(2,128)(2,1)S(1)} %get-tuple-element.109), channel_id=1, source_target_pairs={{0,8},{8,16},{16,24},{1,9},{9,17},{17,25},{2,10},{10,18},{18,26},{... | collective-permute-start | bytes 4616 | tf_op jit(solution)/shard_map/ppermute | solution.py:16
  81.6 4.3 %collective-permute-start.9 = (bf16[2,1,384]{2,1,0:T(2,128)(2,1)S(1)}, bf16[2,1,384]{2,1,0:T(2,128)(2,1)S(1)}, u32[]{:S(2)}, u32[]{:S(2)}) collective-permute-start(bf16[2,1,384]{2,1,0:T(2,128)(2,1)S(1)} %get-tuple-element.110), channel_id=1, source_target_pairs={{8,0},{16,8},{24,16},{9,1},{17,9},{25,17},{10,2},{18,10},{26,18},{... | collective-permute-start | bytes 4616 | tf_op jit(solution)/shard_map/ppermute | solution.py:17
  86.0 9.5 %collective-permute-start.10 = (bf16[1,34,384]{2,1,0:T(8,128)(2,1)S(1)}, bf16[1,34,384]{2,1,0:T(8,128)(2,1)S(1)}, u32[]{:S(2)}, u32[]{:S(2)}) collective-permute-start(bf16[1,34,384]{2,1,0:T(8,128)(2,1)S(1)} %get-tuple-element.107), channel_id=1, source_target_pairs={{0,1},{1,2},{2,3},{3,4},{4,5},{5,6},{6,7},{8,9},{9,10},{10,11},{11... | collective-permute-start | bytes 78344 | tf_op jit(solution)/shard_map/ppermute | solution.py:16
  89.2 6.3 %collective-permute-start.11 = (bf16[1,34,384]{2,1,0:T(8,128)(2,1)S(1)}, bf16[1,34,384]{2,1,0:T(8,128)(2,1)S(1)}, u32[]{:S(2)}, u32[]{:S(2)}) collective-permute-start(bf16[1,34,384]{2,1,0:T(8,128)(2,1)S(1)} %get-tuple-element.108), channel_id=1, source_target_pairs={{1,0},{2,1},{3,2},{4,3},{5,4},{6,5},{7,6},{9,8},{10,9},{11,10},{12... | collective-permute-start | bytes 78344 | tf_op jit(solution)/shard_map/ppermute | solution.py:17
  91.9 14.9 %all-to-all-start = ((bf16[4,2,2,32,384]{4,3,2,1,0:T(8,128)(2,1)}), bf16[4,2,2,32,384]{4,3,2,1,0:T(8,128)(2,1)S(1)}, u32[]{:S(2)}, u32[]{:S(2)}) async-start(bf16[4,2,2,32,384]{4,3,2,1,0:T(8,128)(2,1)} %pad_maximum_fusion.9), calls=%async_computation | async-start | bytes 786432 | tf_op jit(solution)/shard_map/all_to_all | solution.py:86
  95.9 1.0 copy-start.13
  96.2 1.1 copy-start.14
  97.3 16.8 %copy-start.18 = (f32[192]{0:T(256)S(1)}, f32[192]{0:T(256)}, u32[]{:S(2)}) copy-start(f32[192]{0:T(256)} %param.17) | copy-start | bytes 2308
  106.9 8.2 %collective-permute-start.12 = (bf16[2,1,128,384]{3,2,1,0:T(8,128)(2,1)S(1)}, bf16[2,1,128,384]{3,2,1,0:T(8,128)(2,1)S(1)}, u32[]{:S(2)}, u32[]{:S(2)}) collective-permute-start(bf16[2,1,128,384]{3,2,1,0:T(8,128)(2,1)S(1)} %get-tuple-element.96), channel_id=1, source_target_pairs={{0,1},{1,2},{2,3},{3,4},{4,5},{5,6},{6,7},{8,9},{9,10},{10,11},{11... | collective-permute-start | bytes 589832 | tf_op jit(solution)/shard_map/ppermute | solution.py:16
  112.0 7.0 %collective-permute-start.13 = (bf16[2,1,128,384]{3,2,1,0:T(8,128)(2,1)S(1)}, bf16[2,1,128,384]{3,2,1,0:T(8,128)(2,1)S(1)}, u32[]{:S(2)}, u32[]{:S(2)}) collective-permute-start(bf16[2,1,128,384]{3,2,1,0:T(8,128)(2,1)S(1)} %get-tuple-element.97), channel_id=1, source_target_pairs={{1,0},{2,1},{3,2},{4,3},{5,4},{6,5},{7,6},{9,8},{10,9},{11,10},{12... | collective-permute-start | bytes 589832 | tf_op jit(solution)/shard_map/ppermute | solution.py:17
  132.5 2.2 %copy-start.10 = (bf16[1152,192,1,1]{0,1,2,3:T(8,128)(2,1)S(1)}, bf16[1152,192,1,1]{0,1,2,3:T(8,128)(2,1)}, u32[]{:S(2)}) copy-start(bf16[1152,192,1,1]{0,1,2,3:T(8,128)(2,1)} %reshape.105) | copy-start | bytes 1327108
  134.8 2.3 %copy-start.11 = (bf16[1152,192,1,1]{0,1,2,3:T(8,128)(2,1)S(1)}, bf16[1152,192,1,1]{0,1,2,3:T(8,128)(2,1)}, u32[]{:S(2)}) copy-start(bf16[1152,192,1,1]{0,1,2,3:T(8,128)(2,1)} %reshape.107) | copy-start | bytes 1327108
  (4 other events, 4.0 us)
